TPU v7x, 32 devices: a whole 2x2x4 slice. The times are simulated.
32 devices in a mesh: dom: 32 (over z, y, x, core).
Axes of the slice: x: 2, y: 2, z: 4, core: 2. Of those that a mesh axis runs over, the one named last changes fastest.
Arguments:
- particles: float32 [32, 2, 256, 128], P('dom'), may hold values from -60 to 60
- offspring: int32 [32], P('dom'), may hold values from 0 to 7, as said below
- noise: float32 [2, 32, 2, 256, 128], P(None, 'dom'), may hold values from -6 to 6
- accept: int32 [2, 32], P(None, 'dom'), may hold values 0 or 1
- observed: float32 [256, 256], replicated, may hold values from -6 to 6
Outputs:
- moved: float32 [32, 2, 256, 128], P('dom')
- misfit: float32 [2, 32], P(None, 'dom')
Inputs may be any that keep to these rules, and one draw needn't show every extreme that they name: `offspring`: the counts sum to 32. Slot s, numbered by the counts' running sum, is filled by a particle at most 3 places from s, and in every draw some slot is filled from exactly 3 places away.
All inputs are finite; a program needn't handle non-finite values. No bound on the sum of `accept` on one device may be relied on, other than what follows from the above.
Results may differ from a plain program's by a relative error of at most 0.0001.
Values sent between devices are 32-bit elements; how exact they have to be, the bound alone decides.
A program may use at most 64 MiB of HBM per device.

v0:
```python
import math

import jax
import jax.numpy as jnp
from jax import lax
from jax.sharding import PartitionSpec as P

MOVES = 2
SPAN = 3
LOW = 16


time_step = 0.05
viscosity = 0.001
noise_level = 0.5
spectral_scale = 64.0
prior_amplitude = 1.5
step_size = 0.4
highest = lax.Precision.HIGHEST


def from_behind(value, axis, steps):
    count = lax.axis_size(axis)
    leading, last = (max(0, -steps), min(count, count - steps))
    return lax.ppermute(value, axis, [(source, source + steps) for source in range(leading, last)])


def tables(grid):
    half = grid // 2
    index_a = jnp.arange(grid)
    phase_y = (index_a[:, None] * index_a[None, :] % grid).astype(jnp.float32) * (
        2.0 * math.pi / grid
    )
    cos_y = jnp.cos(phase_y)
    sin_y = jnp.sin(phase_y)
    index_q = jnp.arange(half)
    phase_x = (index_q[:, None] * index_a[None, :] % grid).astype(jnp.float32) * (
        2.0 * math.pi / grid
    )
    weight = jnp.where(index_q == 0, 1.0, 2.0).astype(jnp.float32)[:, None]
    backward_table = (
        jnp.concatenate([weight * jnp.cos(phase_x), -weight * jnp.sin(phase_x)], axis=0)
        / spectral_scale
    )
    fore_table = jnp.concatenate([jnp.cos(phase_x).T, -jnp.sin(phase_x).T], axis=1) * (
        spectral_scale / (grid * grid)
    )
    return (cos_y, sin_y, backward_table, fore_table)


def synthesize(real_part, imag_part, lookup_tables):
    cos_y, sin_y, backward_table, fore_table = lookup_tables
    half = real_part.shape[-1]
    stacked = jnp.concatenate([real_part, imag_part], axis=-1)
    with_cos = jnp.einsum("ap,bpq->baq", cos_y, stacked, precision=highest)
    with_sin = jnp.einsum("ap,bpq->baq", sin_y, stacked, precision=highest)
    rows_re = with_cos[..., :half] - with_sin[..., half:]
    rows_im = with_sin[..., :half] + with_cos[..., half:]
    joined = jnp.concatenate([rows_re, rows_im], axis=-1)
    return jnp.einsum("baq,qc->bac", joined, backward_table, precision=highest)


def analyse(field, lookup_tables):
    cos_y, sin_y, backward_table, fore_table = lookup_tables
    half = field.shape[-1] // 2
    rows = jnp.einsum("bac,cq->baq", field, fore_table, precision=highest)
    with_cos = jnp.einsum("ap,baq->bpq", cos_y, rows, precision=highest)
    with_sin = jnp.einsum("ap,baq->bpq", sin_y, rows, precision=highest)
    return (
        with_cos[..., :half] + with_sin[..., half:],
        with_cos[..., half:] - with_sin[..., :half],
    )


def wavenumbers(grid):
    index_y = jnp.arange(grid)
    wave_y = jnp.where(index_y < grid // 2, index_y, index_y - grid).astype(jnp.float32)[:, None]
    wave_x = jnp.arange(grid // 2).astype(jnp.float32)[None, :]
    return (wave_y, wave_x)


def predicted_state(present_state, observed, lookup_tables):
    grid = present_state.shape[2]
    count = present_state.shape[0]
    wave_y, wave_x = wavenumbers(grid)
    wave_sq = wave_y * wave_y + wave_x * wave_x
    inverse_sq = jnp.where(wave_sq > 0, 1.0 / jnp.maximum(wave_sq, 1.0), 0.0)
    keeper = ((jnp.abs(wave_y) <= grid // 3) & (wave_x <= grid // 3)).astype(jnp.float32)
    damping = 1.0 + time_step * viscosity * wave_sq
    real_part = present_state[:, 0]
    imag_part = present_state[:, 1]
    psi_re = real_part * inverse_sq
    psi_im = imag_part * inverse_sq
    fields = synthesize(
        jnp.concatenate([real_part, -wave_y * psi_im, wave_x * psi_im], axis=0),
        jnp.concatenate([imag_part, wave_y * psi_re, -wave_x * psi_re], axis=0),
        lookup_tables,
    )
    vort = fields[:count]
    products = jnp.concatenate(
        [fields[count : 2 * count] * vort, fields[2 * count :] * vort], axis=0
    )
    flux_re, flux_im = analyse(products, lookup_tables)
    nonlin_re = -(wave_x * flux_im[:count] + wave_y * flux_im[count:]) * keeper
    nonlin_im = (wave_x * flux_re[:count] + wave_y * flux_re[count:]) * keeper
    real_part = (real_part - time_step * nonlin_re) / damping
    imag_part = (imag_part - time_step * nonlin_im) / damping
    final = synthesize(real_part, imag_part, lookup_tables)
    return jnp.sum((final - observed[None]) ** 2, axis=(1, 2)) / (
        2.0 * noise_level * noise_level * grid * grid
    )


def low_modes(block):
    grid = block.shape[-2]
    return jnp.concatenate(
        [block[..., : LOW // 2, :LOW], block[..., grid - LOW // 2 :, :LOW]], axis=-2
    )


def body(particles, offspring, noise, accept, observed):
    per_device = particles.shape[0]
    grid = particles.shape[2]
    devices = lax.axis_size("dom")
    position = lax.axis_index("dom")
    every = lax.all_gather(offspring, "dom", axis=0, tiled=True)
    owners = jnp.arange(every.shape[0], dtype=jnp.int32)
    before = jnp.sum(jnp.where(owners < position * per_device, every, 0))
    finish = before + jnp.cumsum(offspring)
    starts = finish - offspring
    package = (particles, starts.astype(jnp.float32), finish.astype(jnp.float32))
    gathered_values = [package]
    for distance in range(1, SPAN + 1):
        for direction in (1, -1):
            gathered_values.append(
                from_behind((package[0], package[1], package[2]), "dom", direction * distance)
            )
    candidates = jnp.concatenate([item[0] for item in gathered_values], axis=0)
    cand_start = jnp.concatenate([item[1] for item in gathered_values], axis=0)
    cand_end = jnp.concatenate([item[2] for item in gathered_values], axis=0)
    slot_ids = (position * per_device + jnp.arange(per_device, dtype=jnp.int32)).astype(jnp.float32)
    chosen = (
        (cand_start[None, :] <= slot_ids[:, None]) & (slot_ids[:, None] < cand_end[None, :])
    ).astype(jnp.float32)
    present_state = jnp.einsum("sc,cxyz->sxyz", chosen, candidates, precision=highest)
    totals = lax.psum(jnp.sum(low_modes(present_state) ** 2, axis=0), "dom")
    adapted = jnp.sqrt(totals / (per_device * devices) + 1e-06)
    wave_y, wave_x = wavenumbers(grid)
    prior = prior_amplitude / (1.0 + jnp.sqrt(wave_y * wave_y + wave_x * wave_x) / 8.0)
    spread = jnp.stack([prior, prior])
    spread = spread.at[:, : LOW // 2, :LOW].set(adapted[:, : LOW // 2])
    spread = spread.at[:, grid - LOW // 2 :, :LOW].set(adapted[:, LOW // 2 :])
    lookup_tables = tables(grid)
    keep = math.sqrt(1.0 - step_size * step_size)
    score_values = []
    for move in range(MOVES):
        candidate_state = keep * present_state + step_size * spread[None] * noise[move]
        score_values.append(predicted_state(candidate_state, observed, lookup_tables))
        present_state = jnp.where(
            accept[move][:, None, None, None] == 1, candidate_state, present_state
        )
    return (present_state, jnp.stack(score_values))


def solution(mesh):
    return jax.shard_map(
        body,
        mesh=mesh,
        in_specs=(
            P("dom", None, None, None),
            P("dom"),
            P(None, "dom", None, None, None),
            P(None, "dom"),
            P(),
        ),
        out_specs=(P("dom", None, None, None), P(None, "dom")),
        check_vma=False,
    )
```

profile of v0, /device:TPU:7, one launch (start us, length us, event | category | flops | bytes accessed | tf_op | source)
XLA Modules:
  0.0 210.9 jit_solution(14020094053850708138)
XLA Ops:
  1.4 39.5 %all-reduce = s32[32]{0:T(128)S(1)} all-reduce(s32[32]{0:T(128)S(1)} %dynamic-update-slice.8), channel_id=1, replica_groups=mesh['dom'=32] {'dom'}, use_global_device_ids=true, to_apply=%add | all-reduce | flops 32 | bytes 256
  42.3 6.1 %collective-permute-start.10 = (f32[1]{0:T(128)}, f32[1]{0:T(128)}, u32[]{:S(2)}, u32[]{:S(2)}) collective-permute-start(f32[1]{0:T(128)} %convert_element_type.176), channel_id=1, source_target_pairs={{0,3},{1,4},{2,5},{3,6},{4,7},{5,8},{6,9},{7,10},{8,11},{9,12},{10... | collective-permute-start | bytes 20 | tf_op jit(solution)/shard_map/ppermute | solution.py:25
  48.4 2.6 %collective-permute-start.11 = (f32[1]{0:T(128)}, f32[1]{0:T(128)}, u32[]{:S(2)}, u32[]{:S(2)}) collective-permute-start(f32[1]{0:T(128)} %convert_element_type.176), channel_id=1, source_target_pairs={{3,0},{4,1},{5,2},{6,3},{7,4},{8,5},{9,6},{10,7},{11,8},{12,9},{13... | collective-permute-start | bytes 20 | tf_op jit(solution)/shard_map/ppermute | solution.py:25
  51.0 4.3 %collective-permute-start.12 = (f32[1,2,256,128]{3,2,1,0:T(8,128)}, f32[1,2,256,128]{3,2,1,0:T(8,128)}, u32[]{:S(2)}, u32[]{:S(2)}) collective-permute-start(f32[1,2,256,128]{3,2,1,0:T(8,128)} %param.9), channel_id=1, source_target_pairs={{0,1},{1,2},{2,3},{3,4},{4,5},{5,6},{6,7},{7,8},{8,9},{9,10},{10,1... | collective-permute-start | bytes 786440 | tf_op jit(solution)/shard_map/ppermute | solution.py:25
  55.3 1.9 collective-permute-start.13
  57.2 3.9 %collective-permute-start.14 = (f32[1,2,256,128]{3,2,1,0:T(8,128)}, f32[1,2,256,128]{3,2,1,0:T(8,128)}, u32[]{:S(2)}, u32[]{:S(2)}) collective-permute-start(f32[1,2,256,128]{3,2,1,0:T(8,128)} %param.9), channel_id=1, source_target_pairs={{0,2},{1,3},{2,4},{3,5},{4,6},{5,7},{6,8},{7,9},{8,10},{9,11},{10,... | collective-permute-start | bytes 786440 | tf_op jit(solution)/shard_map/ppermute | solution.py:25
  67.4 4.6 %collective-permute-start.6 = (f32[1]{0:T(128)}, f32[1]{0:T(128)}, u32[]{:S(2)}, u32[]{:S(2)}) collective-permute-start(f32[1]{0:T(128)} %convert_element_type.176), channel_id=1, source_target_pairs={{0,1},{1,2},{2,3},{3,4},{4,5},{5,6},{6,7},{7,8},{8,9},{9,10},{10,1... | collective-permute-start | bytes 20 | tf_op jit(solution)/shard_map/ppermute | solution.py:25
  72.0 3.0 %collective-permute-start.7 = (f32[1]{0:T(128)}, f32[1]{0:T(128)}, u32[]{:S(2)}, u32[]{:S(2)}) collective-permute-start(f32[1]{0:T(128)} %convert_element_type.176), channel_id=1, source_target_pairs={{1,0},{2,1},{3,2},{4,3},{5,4},{6,5},{7,6},{8,7},{9,8},{10,9},{11,1... | collective-permute-start | bytes 20 | tf_op jit(solution)/shard_map/ppermute | solution.py:25
  75.0 3.6 %collective-permute-start.8 = (f32[1]{0:T(128)}, f32[1]{0:T(128)}, u32[]{:S(2)}, u32[]{:S(2)}) collective-permute-start(f32[1]{0:T(128)} %convert_element_type.176), channel_id=1, source_target_pairs={{0,2},{1,3},{2,4},{3,5},{4,6},{5,7},{6,8},{7,9},{8,10},{9,11},{10,... | collective-permute-start | bytes 20 | tf_op jit(solution)/shard_map/ppermute | solution.py:25
  78.6 3.0 %collective-permute-start.9 = (f32[1]{0:T(128)}, f32[1]{0:T(128)}, u32[]{:S(2)}, u32[]{:S(2)}) collective-permute-start(f32[1]{0:T(128)} %convert_element_type.176), channel_id=1, source_target_pairs={{2,0},{3,1},{4,2},{5,3},{6,4},{7,5},{8,6},{9,7},{10,8},{11,9},{12,... | collective-permute-start | bytes 20 | tf_op jit(solution)/shard_map/ppermute | solution.py:25
  81.7 9.8 %collective-permute-start = (f32[1]{0:T(128)}, f32[1]{0:T(128)}, u32[]{:S(2)}, u32[]{:S(2)}) collective-permute-start(f32[1]{0:T(128)} %convert_element_type.174), channel_id=1, source_target_pairs={{0,1},{1,2},{2,3},{3,4},{4,5},{5,6},{6,7},{7,8},{8,9},{9,10},{10,1... | collective-permute-start | bytes 20 | tf_op jit(solution)/shard_map/ppermute | solution.py:25
  91.5 2.7 %collective-permute-start.1 = (f32[1]{0:T(128)}, f32[1]{0:T(128)}, u32[]{:S(2)}, u32[]{:S(2)}) collective-permute-start(f32[1]{0:T(128)} %convert_element_type.174), channel_id=1, source_target_pairs={{1,0},{2,1},{3,2},{4,3},{5,4},{6,5},{7,6},{8,7},{9,8},{10,9},{11,1... | collective-permute-start | bytes 20 | tf_op jit(solution)/shard_map/ppermute | solution.py:25
  94.2 3.8 %concatenate.77 = f32[7]{0:T(128)S(1)} concatenate(f32[1]{0:T(128)} %convert_element_type.176, f32[1]{0:T(128)} %collective-permute-done.6, f32[1]{0:T(128)} %collective-permute-done.7, f32[1]{0:T(128)} %collective-permute-done.8, f32[1]{0:T(128)} %collective-permute-done.9, f32[1]{0:T(128)} %collective-permute-done.10, f32[1]{0:T(128)} %collective-permute-done.11), dimensions={0} | concatenate | bytes 56 | tf_op jit(solution)/shard_map/concatenate | solution.py:140
  98.0 3.0 %collective-permute-start.2 = (f32[1]{0:T(128)}, f32[1]{0:T(128)}, u32[]{:S(2)}, u32[]{:S(2)}) collective-permute-start(f32[1]{0:T(128)} %convert_element_type.174), channel_id=1, source_target_pairs={{0,2},{1,3},{2,4},{3,5},{4,6},{5,7},{6,8},{7,9},{8,10},{9,11},{10,... | collective-permute-start | bytes 20 | tf_op jit(solution)/shard_map/ppermute | solution.py:25
  101.0 3.7 %collective-permute-start.3 = (f32[1]{0:T(128)}, f32[1]{0:T(128)}, u32[]{:S(2)}, u32[]{:S(2)}) collective-permute-start(f32[1]{0:T(128)} %convert_element_type.174), channel_id=1, source_target_pairs={{2,0},{3,1},{4,2},{5,3},{6,4},{7,5},{8,6},{9,7},{10,8},{11,9},{12,... | collective-permute-start | bytes 20 | tf_op jit(solution)/shard_map/ppermute | solution.py:25
  104.7 6.9 %collective-permute-start.4 = (f32[1]{0:T(128)}, f32[1]{0:T(128)}, u32[]{:S(2)}, u32[]{:S(2)}) collective-permute-start(f32[1]{0:T(128)} %convert_element_type.174), channel_id=1, source_target_pairs={{0,3},{1,4},{2,5},{3,6},{4,7},{5,8},{6,9},{7,10},{8,11},{9,12},{10... | collective-permute-start | bytes 20 | tf_op jit(solution)/shard_map/ppermute | solution.py:25
  111.6 2.6 %collective-permute-start.5 = (f32[1]{0:T(128)}, f32[1]{0:T(128)}, u32[]{:S(2)}, u32[]{:S(2)}) collective-permute-start(f32[1]{0:T(128)} %convert_element_type.174), channel_id=1, source_target_pairs={{3,0},{4,1},{5,2},{6,3},{7,4},{8,5},{9,6},{10,7},{11,8},{12,9},{13... | collective-permute-start | bytes 20 | tf_op jit(solution)/shard_map/ppermute | solution.py:25
  114.2 5.4 %collective-permute-start.15 = (f32[1,2,256,128]{3,2,1,0:T(8,128)}, f32[1,2,256,128]{3,2,1,0:T(8,128)S(1)}, u32[]{:S(2)}, u32[]{:S(2)}) collective-permute-start(f32[1,2,256,128]{3,2,1,0:T(8,128)} %param.9), channel_id=1, source_target_pairs={{2,0},{3,1},{4,2},{5,3},{6,4},{7,5},{8,6},{9,7},{10,8},{11,9},{12,... | collective-permute-start | bytes 786440 | tf_op jit(solution)/shard_map/ppermute | solution.py:25
  119.6 5.4 %collective-permute-start.16 = (f32[1,2,256,128]{3,2,1,0:T(8,128)}, f32[1,2,256,128]{3,2,1,0:T(8,128)}, u32[]{:S(2)}, u32[]{:S(2)}) collective-permute-start(f32[1,2,256,128]{3,2,1,0:T(8,128)} %param.9), channel_id=1, source_target_pairs={{0,3},{1,4},{2,5},{3,6},{4,7},{5,8},{6,9},{7,10},{8,11},{9,12},{10... | collective-permute-start | bytes 786440 | tf_op jit(solution)/shard_map/ppermute | solution.py:25
  125.0 3.7 %concatenate.76 = f32[7]{0:T(128)S(1)} concatenate(f32[1]{0:T(128)} %convert_element_type.174, f32[1]{0:T(128)} %collective-permute-done, f32[1]{0:T(128)} %collective-permute-done.1, f32[1]{0:T(128)} %collective-permute-done.2, f32[1]{0:T(128)} %collective-permute-done.3, f32[1]{0:T(128)} %collective-permute-done.4, f32[1]{0:T(128)} %collective-permute-done.5), dimensions={0} | concatenate | bytes 56 | tf_op jit(solution)/shard_map/concatenate | solution.py:139
  134.6 4.1 %collective-permute-done.17 = f32[1,2,256,128]{3,2,1,0:T(8,128)S(1)} collective-permute-done((f32[1,2,256,128]{3,2,1,0:T(8,128)}, f32[1,2,256,128]{3,2,1,0:T(8,128)S(1)}, u32[]{:S(2)}, u32[]{:S(2)}) %collective-permute-start.17) | collective-permute-done | bytes 262176 | tf_op jit(solution)/shard_map/ppermute | solution.py:25
  138.7 2.0 fusion
  141.0 38.2 %psum.7 = f32[2,16,16]{1,2,0:T(8,128)S(1)} all-reduce(f32[2,16,16]{1,2,0:T(8,128)S(1)} %maximum_multiply_fusion.6), channel_id=1, replica_groups=mesh['dom'=32] {'dom'}, use_global_device_ids=true, to_apply=%region_1.2 | all-reduce | flops 512 | bytes 4096 | tf_op jit(solution)/shard_map/psum | solution.py:146
  192.4 2.0 convolution_bitcast_fusion.2
  (88 shorter events, 39.1 us)
Async XLA Ops:
  0.6 63.3 %copy-start.1 = (s32[2,1]{0,1:T(1,128)S(1)}, s32[2,1]{0,1:T(1,128)}, u32[]{:S(2)}) copy-start(s32[2,1]{0,1:T(1,128)} %param.12) | copy-start | bytes 28
  42.3 25.1 %collective-permute-start.10 = (f32[1]{0:T(128)}, f32[1]{0:T(128)}, u32[]{:S(2)}, u32[]{:S(2)}) collective-permute-start(f32[1]{0:T(128)} %convert_element_type.176), channel_id=1, source_target_pairs={{0,3},{1,4},{2,5},{3,6},{4,7},{5,8},{6,9},{7,10},{8,11},{9,12},{10... | collective-permute-start | bytes 20 | tf_op jit(solution)/shard_map/ppermute | solution.py:25
  48.4 23.6 %collective-permute-start.11 = (f32[1]{0:T(128)}, f32[1]{0:T(128)}, u32[]{:S(2)}, u32[]{:S(2)}) collective-permute-start(f32[1]{0:T(128)} %convert_element_type.176), channel_id=1, source_target_pairs={{3,0},{4,1},{5,2},{6,3},{7,4},{8,5},{9,6},{10,7},{11,8},{12,9},{13... | collective-permute-start | bytes 20 | tf_op jit(solution)/shard_map/ppermute | solution.py:25
  51.0 77.7 %collective-permute-start.12 = (f32[1,2,256,128]{3,2,1,0:T(8,128)}, f32[1,2,256,128]{3,2,1,0:T(8,128)}, u32[]{:S(2)}, u32[]{:S(2)}) collective-permute-start(f32[1,2,256,128]{3,2,1,0:T(8,128)} %param.9), channel_id=1, source_target_pairs={{0,1},{1,2},{2,3},{3,4},{4,5},{5,6},{6,7},{7,8},{8,9},{9,10},{10,1... | collective-permute-start | bytes 786440 | tf_op jit(solution)/shard_map/ppermute | solution.py:25
  55.3 76.3 %collective-permute-start.13 = (f32[1,2,256,128]{3,2,1,0:T(8,128)}, f32[1,2,256,128]{3,2,1,0:T(8,128)}, u32[]{:S(2)}, u32[]{:S(2)}) collective-permute-start(f32[1,2,256,128]{3,2,1,0:T(8,128)} %param.9), channel_id=1, source_target_pairs={{1,0},{2,1},{3,2},{4,3},{5,4},{6,5},{7,6},{8,7},{9,8},{10,9},{11,1... | collective-permute-start | bytes 786440 | tf_op jit(solution)/shard_map/ppermute | solution.py:25
  57.2 75.4 %collective-permute-start.14 = (f32[1,2,256,128]{3,2,1,0:T(8,128)}, f32[1,2,256,128]{3,2,1,0:T(8,128)}, u32[]{:S(2)}, u32[]{:S(2)}) collective-permute-start(f32[1,2,256,128]{3,2,1,0:T(8,128)} %param.9), channel_id=1, source_target_pairs={{0,2},{1,3},{2,4},{3,5},{4,6},{5,7},{6,8},{7,9},{8,10},{9,11},{10,... | collective-permute-start | bytes 786440 | tf_op jit(solution)/shard_map/ppermute | solution.py:25
  67.4 7.6 %collective-permute-start.6 = (f32[1]{0:T(128)}, f32[1]{0:T(128)}, u32[]{:S(2)}, u32[]{:S(2)}) collective-permute-start(f32[1]{0:T(128)} %convert_element_type.176), channel_id=1, source_target_pairs={{0,1},{1,2},{2,3},{3,4},{4,5},{5,6},{6,7},{7,8},{8,9},{9,10},{10,1... | collective-permute-start | bytes 20 | tf_op jit(solution)/shard_map/ppermute | solution.py:25
  72.0 6.6 %collective-permute-start.7 = (f32[1]{0:T(128)}, f32[1]{0:T(128)}, u32[]{:S(2)}, u32[]{:S(2)}) collective-permute-start(f32[1]{0:T(128)} %convert_element_type.176), channel_id=1, source_target_pairs={{1,0},{2,1},{3,2},{4,3},{5,4},{6,5},{7,6},{8,7},{9,8},{10,9},{11,1... | collective-permute-start | bytes 20 | tf_op jit(solution)/shard_map/ppermute | solution.py:25
  75.0 6.7 %collective-permute-start.8 = (f32[1]{0:T(128)}, f32[1]{0:T(128)}, u32[]{:S(2)}, u32[]{:S(2)}) collective-permute-start(f32[1]{0:T(128)} %convert_element_type.176), channel_id=1, source_target_pairs={{0,2},{1,3},{2,4},{3,5},{4,6},{5,7},{6,8},{7,9},{8,10},{9,11},{10,... | collective-permute-start | bytes 20 | tf_op jit(solution)/shard_map/ppermute | solution.py:25
  78.6 12.9 %collective-permute-start.9 = (f32[1]{0:T(128)}, f32[1]{0:T(128)}, u32[]{:S(2)}, u32[]{:S(2)}) collective-permute-start(f32[1]{0:T(128)} %convert_element_type.176), channel_id=1, source_target_pairs={{2,0},{3,1},{4,2},{5,3},{6,4},{7,5},{8,6},{9,7},{10,8},{11,9},{12,... | collective-permute-start | bytes 20 | tf_op jit(solution)/shard_map/ppermute | solution.py:25
  81.7 16.3 %collective-permute-start = (f32[1]{0:T(128)}, f32[1]{0:T(128)}, u32[]{:S(2)}, u32[]{:S(2)}) collective-permute-start(f32[1]{0:T(128)} %convert_element_type.174), channel_id=1, source_target_pairs={{0,1},{1,2},{2,3},{3,4},{4,5},{5,6},{6,7},{7,8},{8,9},{9,10},{10,1... | collective-permute-start | bytes 20 | tf_op jit(solution)/shard_map/ppermute | solution.py:25
  91.5 9.4 %collective-permute-start.1 = (f32[1]{0:T(128)}, f32[1]{0:T(128)}, u32[]{:S(2)}, u32[]{:S(2)}) collective-permute-start(f32[1]{0:T(128)} %convert_element_type.174), channel_id=1, source_target_pairs={{1,0},{2,1},{3,2},{4,3},{5,4},{6,5},{7,6},{8,7},{9,8},{10,9},{11,1... | collective-permute-start | bytes 20 | tf_op jit(solution)/shard_map/ppermute | solution.py:25
  98.0 6.7 %collective-permute-start.2 = (f32[1]{0:T(128)}, f32[1]{0:T(128)}, u32[]{:S(2)}, u32[]{:S(2)}) collective-permute-start(f32[1]{0:T(128)} %convert_element_type.174), channel_id=1, source_target_pairs={{0,2},{1,3},{2,4},{3,5},{4,6},{5,7},{6,8},{7,9},{8,10},{9,11},{10,... | collective-permute-start | bytes 20 | tf_op jit(solution)/shard_map/ppermute | solution.py:25
  101.0 10.6 %collective-permute-start.3 = (f32[1]{0:T(128)}, f32[1]{0:T(128)}, u32[]{:S(2)}, u32[]{:S(2)}) collective-permute-start(f32[1]{0:T(128)} %convert_element_type.174), channel_id=1, source_target_pairs={{2,0},{3,1},{4,2},{5,3},{6,4},{7,5},{8,6},{9,7},{10,8},{11,9},{12,... | collective-permute-start | bytes 20 | tf_op jit(solution)/shard_map/ppermute | solution.py:25
  104.7 9.5 %collective-permute-start.4 = (f32[1]{0:T(128)}, f32[1]{0:T(128)}, u32[]{:S(2)}, u32[]{:S(2)}) collective-permute-start(f32[1]{0:T(128)} %convert_element_type.174), channel_id=1, source_target_pairs={{0,3},{1,4},{2,5},{3,6},{4,7},{5,8},{6,9},{7,10},{8,11},{9,12},{10... | collective-permute-start | bytes 20 | tf_op jit(solution)/shard_map/ppermute | solution.py:25
  111.6 8.1 %collective-permute-start.5 = (f32[1]{0:T(128)}, f32[1]{0:T(128)}, u32[]{:S(2)}, u32[]{:S(2)}) collective-permute-start(f32[1]{0:T(128)} %convert_element_type.174), channel_id=1, source_target_pairs={{3,0},{4,1},{5,2},{6,3},{7,4},{8,5},{9,6},{10,7},{11,8},{12,9},{13... | collective-permute-start | bytes 20 | tf_op jit(solution)/shard_map/ppermute | solution.py:25
  114.2 19.4 %collective-permute-start.15 = (f32[1,2,256,128]{3,2,1,0:T(8,128)}, f32[1,2,256,128]{3,2,1,0:T(8,128)S(1)}, u32[]{:S(2)}, u32[]{:S(2)}) collective-permute-start(f32[1,2,256,128]{3,2,1,0:T(8,128)} %param.9), channel_id=1, source_target_pairs={{2,0},{3,1},{4,2},{5,3},{6,4},{7,5},{8,6},{9,7},{10,8},{11,9},{12,... | collective-permute-start | bytes 786440 | tf_op jit(solution)/shard_map/ppermute | solution.py:25
  119.6 14.0 %collective-permute-start.16 = (f32[1,2,256,128]{3,2,1,0:T(8,128)}, f32[1,2,256,128]{3,2,1,0:T(8,128)}, u32[]{:S(2)}, u32[]{:S(2)}) collective-permute-start(f32[1,2,256,128]{3,2,1,0:T(8,128)} %param.9), channel_id=1, source_target_pairs={{0,3},{1,4},{2,5},{3,6},{4,7},{5,8},{6,9},{7,10},{8,11},{9,12},{10... | collective-permute-start | bytes 786440 | tf_op jit(solution)/shard_map/ppermute | solution.py:25
  128.7 9.9 %collective-permute-start.17 = (f32[1,2,256,128]{3,2,1,0:T(8,128)}, f32[1,2,256,128]{3,2,1,0:T(8,128)S(1)}, u32[]{:S(2)}, u32[]{:S(2)}) collective-permute-start(f32[1,2,256,128]{3,2,1,0:T(8,128)} %param.9), channel_id=1, source_target_pairs={{3,0},{4,1},{5,2},{6,3},{7,4},{8,5},{9,6},{10,7},{11,8},{12,9},{13... | collective-permute-start | bytes 786440 | tf_op jit(solution)/shard_map/ppermute | solution.py:25
  202.9 2.8 %copy-start = (f32[256,256]{1,0:T(8,128)S(1)}, f32[256,256]{1,0:T(8,128)}, u32[]{:S(2)}) copy-start(f32[256,256]{1,0:T(8,128)} %param.13) | copy-start | bytes 786436
where the time goes:
time: 214 us; the launch traced here: 211 us
  blocking collectives  77.8 us (36%)
  starting transfers between devices  74.6 us (35%)
  matrix products  27.5 us (13%)
  local copies, waits for them, and re-layouts  17.5 us (8%)
  between operations  5.73 us (3%)
  waiting for transfers between devices  4.1 us (2%)
  other arithmetic  3.6 us (2%)
    ppermute x18, starting transfers between devices, from_behind(): lax.ppermute(value, axis, [(source, source + steps) for source in range(l...  74.6 us
    unnamed x1, blocking collectives  39.5 us
    psum x1, blocking collectives, body(): totals = lax.psum(jnp.sum(low_modes(present_state) ** 2, axis=0), 'dom')  38.2 us
    dot_general x4, matrix products, synthesize(): with_sin = jnp.einsum('ap,bpq->baq', sin_y, stacked, precision=highest)  6.48 us
    dot_general x4, matrix products, synthesize(): with_cos = jnp.einsum('ap,bpq->baq', cos_y, stacked, precision=highest)  6.22 us
    unnamed x15, local copies, waits for them, and re-layouts  6.1 us
    dot_general x4, matrix products, synthesize(): return jnp.einsum('baq,qc->bac', joined, backward_table, precision=highest)  5.23 us
  transfers between devices with their start and end apart: 18, of which 1 were waited for; matrix products, arithmetic and copies ran while one was open for 7% of the time, Pallas kernels for 0%

commit v1 on v0

v1 whole, which is shorter than its diff:
```python
import functools
import math

import jax
import jax.numpy as jnp
import ml_dtypes
import numpy as np
from jax import lax
from jax.experimental import pallas as pl
from jax.experimental.pallas import tpu as pltpu
from jax.sharding import PartitionSpec as P

REACH = 3
LOW = 16
LANES = 128
COUNT_ROWS = 8
PARTS = 2
GROUP_BITS = 3

time_step = 0.05
viscosity = 0.001
noise_level = 0.5
spectral_scale = 64.0
prior_amplitude = 1.5
step_size = 0.4

MESH = pl.DeviceIdType.MESH


def split_bits(devices):
    bits = devices.bit_length() - 1
    assert 1 << bits == devices
    groups = []
    first = 0
    while first < bits:
        width = min(GROUP_BITS, bits - first)
        groups.append((first, width))
        first += width
    return groups


def exchange_kernel(
    devices, groups, x_ref, count_ref, picked_ref, total_ref,
    cand, sums, small, load_sem, big_send, big_recv, small_send, small_recv,
):
    grid = x_ref.shape[2]
    me = lax.axis_index("dom")
    core = lax.rem(me, 2)
    sibling = me + 1 - 2 * core
    left, right = me - 2, me + 2
    has_left, has_right = me >= 2, me + 2 < devices
    far = me - 3 + 6 * core
    has_far = jnp.logical_and(far >= 0, far < devices)

    load = pltpu.make_async_copy(x_ref.at[0], cand.at[REACH], load_sem)
    load.start()

    barrier = pltpu.get_barrier_semaphore()

    def greet(device):
        pl.semaphore_signal(barrier, inc=1, device_id=(device,), device_id_type=MESH)

    partners = []
    for first, width in groups:
        partners.append([jnp.bitwise_xor(me, k << first) for k in range(1, 1 << width)])
    for group in partners:
        for device in group:
            greet(device)
    pl.when(has_left)(lambda: greet(left))
    pl.when(has_right)(lambda: greet(right))
    pl.when(has_far)(lambda: greet(far))

    load.wait()
    count = count_ref[0].astype(jnp.float32)
    half_low = LOW // 2
    for part in range(PARTS):
        for at, start in enumerate((0, grid - half_low)):
            block = cand[REACH, part, start : start + half_low, :]
            row = (2 * part + at) * half_low
            sums[0, row : row + half_low, :] = block * block * count
    row_ids = lax.broadcasted_iota(jnp.int32, (COUNT_ROWS, LANES), 0)
    lane_ids = lax.broadcasted_iota(jnp.int32, (COUNT_ROWS, LANES), 1)
    order = row_ids * LANES + lane_ids
    sums[0, PARTS * LOW :, :] = jnp.where(order == me, count, 0.0)

    expected = sum(len(group) for group in partners)
    expected = expected + has_left.astype(jnp.int32) + has_right.astype(jnp.int32) + has_far.astype(jnp.int32)
    pl.semaphore_wait(barrier, expected)

    def stage_copies(stage):
        copies = []
        base = sum(len(group) for group in partners[:stage])
        for at, device in enumerate(partners[stage]):
            copies.append(
                pltpu.make_async_remote_copy(
                    src_ref=sums.at[stage],
                    dst_ref=small.at[base + at],
                    send_sem=small_send.at[base + at],
                    recv_sem=small_recv.at[base + at],
                    device_id=(device,),
                    device_id_type=MESH,
                )
            )
        return copies

    def big_copy(source, target, piece, send_at, device):
        return pltpu.make_async_remote_copy(
            src_ref=cand.at[source, piece],
            dst_ref=cand.at[target, piece],
            send_sem=big_send.at[send_at, piece],
            recv_sem=big_recv.at[target, piece],
            device_id=(device,),
            device_id_type=MESH,
        )

    own = REACH
    sends = []
    for piece in range(PARTS):
        sends.append((has_right, big_copy(own, 1, piece, 0, right)))
        sends.append((has_left, big_copy(own, 5, piece, 1, left)))
    for piece in range(PARTS):
        sends.append((has_far, big_copy(own, 6 - 6 * core, piece, 2, far)))
    for piece in range(PARTS):
        sends.append((None, big_copy(own, 2 + 2 * core, piece, 3, sibling)))
    relays = []
    for piece in range(PARTS):
        relays.append((has_left, big_copy(1, 2 * core, piece, 4, sibling), (1, piece)))
        relays.append((has_right, big_copy(5, 4 + 2 * core, piece, 5, sibling), (5, piece)))

    def arrived(slot, piece):
        big_copy(slot, slot, piece, 0, sibling).wait_recv()

    first_stage = stage_copies(0)
    for copy in first_stage:
        copy.start()
    for test, copy in sends:
        if test is None:
            copy.start()
        else:
            pl.when(test)(copy.start)

    for stage in range(len(groups)):
        copies = first_stage if stage == 0 else stage_copies(stage)
        if stage > 0:
            for copy in copies:
                copy.start()
        for copy in copies:
            copy.wait_recv()
        base = sum(len(group) for group in partners[:stage])
        total = sums[stage]
        for at in range(len(copies)):
            total = total + small[base + at]
        sums[stage + 1] = total
        for copy in copies:
            copy.wait_send()

    counts = sums[len(groups), PARTS * LOW :, :]
    total_ref[...] = sums[len(groups), : PARTS * LOW, :]
    shift = jnp.full((1, 1), -float(REACH), jnp.float32)
    slot = me.astype(jnp.float32)
    for distance in range(-REACH, REACH):
        ends = jnp.sum(jnp.where(order <= me + distance, counts, 0.0), keepdims=True)
        shift = shift + jnp.where(ends <= slot, 1.0, 0.0)

    for test, copy, (slot_at, piece) in relays:
        @pl.when(test)
        def _():
            arrived(slot_at, piece)
            copy.start()

    for piece in range(PARTS):
        arrived(4 - 2 * core, piece)

        @pl.when(has_left)
        def _():
            arrived(2 - 2 * core, piece)

        @pl.when(has_right)
        def _():
            arrived(6 - 2 * core, piece)

        @pl.when(has_far)
        def _():
            arrived(6 * core, piece)

    rows = 32
    choice = jnp.broadcast_to(shift, (rows, LANES))

    for part in range(PARTS):
        def pick(at, carry):
            span = pl.ds(pl.multiple_of(at * rows, rows), rows)
            value = cand[REACH, part, span, :]
            for distance in range(-REACH, REACH + 1):
                if distance != 0:
                    value = jnp.where(choice == distance, cand[REACH + distance, part, span, :], value)
            picked_ref[part, span, :] = value
            return carry

        lax.fori_loop(0, grid // rows, pick, 0)

    for test, copy in sends:
        if test is None:
            copy.wait_send()
        else:
            pl.when(test)(copy.wait_send)
    for test, copy, _ in relays:
        pl.when(test)(copy.wait_send)


def exchange(particles, offspring, devices):
    groups = split_bits(devices)
    _, _, grid, half = particles.shape
    assert particles.shape[0] == 1 and half == LANES and devices <= COUNT_ROWS * LANES
    copies = sum((1 << width) - 1 for _, width in groups)
    package = PARTS * LOW + COUNT_ROWS
    slots = 2 * REACH + 1
    return pl.pallas_call(
        functools.partial(exchange_kernel, devices, groups),
        out_shape=(
            jax.ShapeDtypeStruct((PARTS, grid, half), jnp.float32),
            jax.ShapeDtypeStruct((PARTS * LOW, LANES), jnp.float32),
        ),
        in_specs=[
            pl.BlockSpec(memory_space=pl.ANY),
            pl.BlockSpec(memory_space=pltpu.SMEM),
        ],
        out_specs=(
            pl.BlockSpec(memory_space=pltpu.VMEM),
            pl.BlockSpec(memory_space=pltpu.VMEM),
        ),
        scratch_shapes=[
            pltpu.VMEM((slots, PARTS, grid, half), jnp.float32),
            pltpu.VMEM((len(groups) + 1, package, LANES), jnp.float32),
            pltpu.VMEM((copies, package, LANES), jnp.float32),
            pltpu.SemaphoreType.DMA,
            pltpu.SemaphoreType.DMA((6, PARTS)),
            pltpu.SemaphoreType.DMA((slots, PARTS)),
            pltpu.SemaphoreType.DMA((copies,)),
            pltpu.SemaphoreType.DMA((copies,)),
        ],
        compiler_params=pltpu.CompilerParams(
            collective_id=0, has_side_effects=True, vmem_limit_bytes=16 * 1024 * 1024
        ),
        name="exchange",
    )(particles, offspring)


def halves(table):
    table = np.asarray(table, np.float64)
    high = table.astype(np.float32).astype(ml_dtypes.bfloat16)
    rest = (table - high.astype(np.float64)).astype(np.float32).astype(ml_dtypes.bfloat16)
    return np.stack([high, rest])


def make_tables(grid):
    half = grid // 2
    angle = 2.0 * math.pi / grid
    index = np.arange(grid)
    low = np.arange(half)
    phase = (index[:, None] * low[None, :] % grid) * angle
    sines = np.sin(phase)
    sines[:, 0] = 1.0 - 2.0 * (index % 2)
    fold = np.concatenate([np.cos(phase), sines], axis=1)
    weight = np.where(low == 0, 1.0, 2.0)[:, None]
    back = np.concatenate([weight * np.cos(phase).T, -weight * np.sin(phase).T], axis=0) / spectral_scale
    fore = np.concatenate([np.cos(phase), -np.sin(phase)], axis=1) * (spectral_scale / (grid * grid))
    flip = np.zeros((half, half))
    flip[low, (half - low) % half] = 1.0
    wave_y = np.concatenate([low, np.where(low == 0, half, low)]).astype(np.float64)[:, None]
    wave_x = low.astype(np.float64)[None, :]
    square = wave_y**2 + wave_x**2
    inverse = np.where(square > 0, 1.0 / np.maximum(square, 1.0), 0.0)
    damping = 1.0 / (1.0 + time_step * viscosity * square)
    keeper = (np.abs(wave_y) <= grid // 3) & (wave_x <= grid // 3)
    doubled = np.where(np.concatenate([low, low])[:, None] == 0, 1.0, 2.0)
    flux = -time_step * keeper * doubled * damping
    signed = np.where(index < half, index, index - grid).astype(np.float64)[:, None]
    prior = prior_amplitude / (1.0 + np.sqrt(signed**2 + wave_x**2) / 8.0)
    scales = np.stack([inverse, damping, flux, step_size * prior]).astype(np.float32)
    return (
        halves(fold), halves(fold.T), halves(back), halves(fore),
        flip.astype(ml_dtypes.bfloat16), scales,
    )


def split(value):
    high = value.astype(jnp.bfloat16)
    return high, (value - high.astype(jnp.float32)).astype(jnp.bfloat16)


def dot(a, b):
    return jnp.dot(a, b, preferred_element_type=jnp.float32)


def table_left(table, value):
    high, rest = split(value)
    return dot(table[0], high) + dot(table[0], rest) + dot(table[1], high)


def table_right(value, table):
    high, rest = split(value)
    return dot(high, table[0]) + dot(rest, table[0]) + dot(high, table[1])


def moves_kernel(
    devices, picked_ref, total_ref, noise_ref, accept_ref, observed_ref,
    fold_ref, unfold_ref, back_ref, fore_ref, flip_ref, scale_ref,
    moved_ref, misfit_ref,
):
    _, grid, half = picked_ref.shape
    moves = noise_ref.shape[0]
    half_low = LOW // 2
    keep = math.sqrt(1.0 - step_size * step_size)

    lanes = lax.broadcasted_iota(jnp.int32, (half_low, half), 1)

    def spread(part):
        prior = scale_ref[3]
        top, bottom = prior[:half_low], prior[grid - half_low :]
        total = total_ref[part * LOW : (part + 1) * LOW, :]
        adapted = step_size * jnp.sqrt(total * (1.0 / devices) + 1e-06)
        top = jnp.where(lanes < LOW, adapted[:half_low], top)
        bottom = jnp.where(lanes < LOW, adapted[half_low:], bottom)
        return jnp.concatenate([top, prior[half_low : grid - half_low], bottom], axis=0)

    spreads = [spread(part) for part in range(PARTS)]
    present = [picked_ref[part] for part in range(PARTS)]
    proposals = []
    for move in range(moves):
        taken = accept_ref[move, 0] == 1
        candidate = [keep * present[part] + spreads[part] * noise_ref[move, 0, part] for part in range(PARTS)]
        present = [jnp.where(taken, candidate[part], present[part]) for part in range(PARTS)]
        proposals.append(candidate)
    for part in range(PARTS):
        moved_ref[0, part] = present[part]

    row_ids = lax.broadcasted_iota(jnp.int32, (half, grid), 0)
    first = row_ids == 0
    wave = row_ids.astype(jnp.float32)
    wave_x = lax.broadcasted_iota(jnp.int32, (grid, half), 1).astype(jnp.float32)
    fold = (fold_ref[0], fold_ref[1])
    unfold = (unfold_ref[0], unfold_ref[1])
    back = (back_ref[0], back_ref[1])
    fore = (fore_ref[0], fore_ref[1])
    flip = flip_ref[...]

    def wide(index):
        value = scale_ref[index]
        return jnp.concatenate([value, value], axis=1)

    def turn(value):
        return jnp.concatenate([-value[:, half:], value[:, :half]], axis=1)

    states = []
    for real_part, imag_part in proposals:
        top = jnp.concatenate([real_part[:half], imag_part[:half]], axis=1)
        high, rest = split(jnp.concatenate([real_part[half:], imag_part[half:]], axis=1))
        other = dot(flip, high) + dot(flip, rest)
        even = top + jnp.where(first, 0.0, other)
        odd = jnp.where(first, other, turn(top - other))
        states.append(jnp.concatenate([even, odd], axis=0))

    inverse = wide(0)
    rows = []
    for state in states:
        psi = state * inverse
        psi_even, psi_odd = psi[:half], psi[half:]
        along_y = jnp.concatenate(
            [wave * psi_odd, jnp.where(first, -float(half) * turn(psi_odd), -wave * psi_even)], axis=0
        )
        along_x = jnp.concatenate([wave_x * psi[:, half:], -wave_x * psi[:, :half]], axis=1)
        for value in (state, along_y, along_x):
            rows.append(table_left(fold, value))
    fields = table_right(jnp.concatenate(rows, axis=0), back)

    products = []
    for move in range(moves):
        vort = fields[(3 * move) * grid : (3 * move + 1) * grid]
        for at in (1, 2):
            products.append(fields[(3 * move + at) * grid : (3 * move + at + 1) * grid] * vort)
    flux_rows = table_right(jnp.concatenate(products, axis=0), fore)

    damping = wide(1)
    flux_scale = wide(2)
    finals = []
    for move in range(moves):
        flux_u = table_left(unfold, flux_rows[(2 * move) * grid : (2 * move + 1) * grid])
        flux_v = table_left(unfold, flux_rows[(2 * move + 1) * grid : (2 * move + 2) * grid])
        along_x = jnp.concatenate([-wave_x * flux_u[:, half:], wave_x * flux_u[:, :half]], axis=1)
        along_y = jnp.concatenate([wave * flux_v[half:], -wave * flux_v[:half]], axis=0)
        state = states[move] * damping + flux_scale * (along_x + along_y)
        finals.append(table_left(fold, state))
    forecast = table_right(jnp.concatenate(finals, axis=0), back)
    for move in range(moves):
        gap = forecast[move * grid : (move + 1) * grid] - observed_ref[...]
        misfit_ref[move, 0] = jnp.sum(gap * gap) * (1.0 / (2.0 * noise_level * noise_level * grid * grid))


def apply_moves(picked, totals, noise, accept, observed, devices):
    _, grid, half = picked.shape
    moves = noise.shape[0]
    tables = [jnp.asarray(table) for table in make_tables(grid)]
    flops = 2 * moves * 36 * grid**3
    vmem = pl.BlockSpec(memory_space=pltpu.VMEM)
    smem = pl.BlockSpec(memory_space=pltpu.SMEM)
    return pl.pallas_call(
        functools.partial(moves_kernel, devices),
        out_shape=(
            jax.ShapeDtypeStruct((1, PARTS, grid, half), jnp.float32),
            jax.ShapeDtypeStruct((moves, 1), jnp.float32),
        ),
        in_specs=[vmem, vmem, vmem, smem] + [vmem] * 7,
        out_specs=(vmem, smem),
        cost_estimate=pl.CostEstimate(flops=flops, bytes_accessed=4 * 1024 * 1024, transcendentals=0),
        compiler_params=pltpu.CompilerParams(vmem_limit_bytes=40 * 1024 * 1024),
        name="moves",
    )(picked, totals, noise, accept, observed, *tables)


def body(devices, particles, offspring, noise, accept, observed):
    picked, totals = exchange(particles, offspring, devices)
    return apply_moves(picked, totals, noise, accept, observed, devices)


def solution(mesh):
    return jax.shard_map(
        functools.partial(body, mesh.shape["dom"]),
        mesh=mesh,
        in_specs=(
            P("dom", None, None, None),
            P("dom"),
            P(None, "dom", None, None, None),
            P(None, "dom"),
            P(),
        ),
        out_specs=(P("dom", None, None, None), P(None, "dom")),
        check_vma=False,
    )
```

time: 214 us -> 39.4 us (0.18)
  the two profiles are of different devices: /device:TPU:7 before, /device:TPU:1 now
where the time goes in v1:
time: 39.4 us; the launch traced here: 39 us
  Pallas kernels  29.4 us (75%)
  local copies, waits for them, and re-layouts  8.28 us (21%)
  between operations  1.35 us (3%)
    pallas_call x1, Pallas kernels, exchange(): pl.pallas_call(functools.partial(exchange_kernel, devices, groups), out_s...  23.6 us
    unnamed x21, local copies, waits for them, and re-layouts  7.68 us
    pallas_call x1, Pallas kernels, apply_moves(): pl.pallas_call(functools.partial(moves_kernel, devices), out_shape=(jax.S...  5.77 us

profile of v1, /device:TPU:1, one launch (start us, length us, event | category | flops | bytes accessed | tf_op | source)
XLA Modules:
  0.0 39.0 jit_solution(10217489660565365293)
XLA Ops:
  0.6 0.0 copy-start.9
  1.3 0.0 copy-done.9
  1.3 0.1 copy.13.accept_ref
  1.4 0.0 copy-start
  1.4 0.9 %copy-done = f32[1,2,256,128]{3,2,1,0:T(8,128)S(1)} copy-done((f32[1,2,256,128]{3,2,1,0:T(8,128)S(1)}, f32[1,2,256,128]{3,2,1,0:T(8,128)}, u32[]{:S(2)}) %copy-start) | copy-done | bytes 262168
  2.4 0.0 copy-start.2
  2.4 23.6 %exchange.1 = (f32[2,256,128]{2,1,0:T(8,128)S(1)}, f32[32,128]{1,0:T(8,128)S(1)}) custom-call(f32[1,2,256,128]{3,2,1,0:T(8,128)S(1)} %copy-done, s32[1]{0:T(128)S(6)} %copy.15.count_ref), custom_call_target="tpu_custom_call" | custom-call | tf_op jit(solution)/shard_map/exchange/pallas_call | solution.py:217
  25.9 0.0 copy-done.2
  26.0 0.0 copy-start.1
  26.0 1.0 %copy-done.1 = f32[2,1,2,256,128]{4,3,2,1,0:T(8,128)S(1)} copy-done((f32[2,1,2,256,128]{4,3,2,1,0:T(8,128)S(1)}, f32[2,1,2,256,128]{4,3,2,1,0:T(8,128)}, u32[]{:S(2)}) %copy-start.1) | copy-done | bytes 524312
  27.0 0.0 copy-start.3
  27.0 1.0 %copy-done.3 = f32[4,256,128]{2,1,0:T(8,128)S(1)} copy-done((f32[4,256,128]{2,1,0:T(8,128)S(1)}, f32[4,256,128]{2,1,0:T(8,128)}, u32[]{:S(2)}) %copy-start.3) | copy-done | bytes 524312
  28.0 0.0 copy-start.4
  28.0 0.9 %copy-done.4 = bf16[2,256,256]{2,1,0:T(8,128)(2,1)S(1)} copy-done((bf16[2,256,256]{2,1,0:T(8,128)(2,1)S(1)}, bf16[2,256,256]{2,1,0:T(8,128)(2,1)}, u32[]{:S(2)}) %copy-start.4) | copy-done | bytes 262168
  29.0 0.0 copy-start.5
  29.0 0.9 %copy-done.5 = bf16[2,256,256]{2,1,0:T(8,128)(2,1)S(1)} copy-done((bf16[2,256,256]{2,1,0:T(8,128)(2,1)S(1)}, bf16[2,256,256]{2,1,0:T(8,128)(2,1)}, u32[]{:S(2)}) %copy-start.5) | copy-done | bytes 262168
  29.9 0.0 copy-start.6
  29.9 0.9 %copy-done.6 = bf16[2,256,256]{2,1,0:T(8,128)(2,1)S(1)} copy-done((bf16[2,256,256]{2,1,0:T(8,128)(2,1)S(1)}, bf16[2,256,256]{2,1,0:T(8,128)(2,1)}, u32[]{:S(2)}) %copy-start.6) | copy-done | bytes 262168
  30.9 0.0 copy-start.7
  30.9 0.9 %copy-done.7 = bf16[2,256,256]{2,1,0:T(8,128)(2,1)S(1)} copy-done((bf16[2,256,256]{2,1,0:T(8,128)(2,1)S(1)}, bf16[2,256,256]{2,1,0:T(8,128)(2,1)}, u32[]{:S(2)}) %copy-start.7) | copy-done | bytes 262168
  31.8 0.0 copy-start.8
  31.8 0.8 %copy-done.8 = bf16[128,128]{1,0:T(8,128)(2,1)S(1)} copy-done((bf16[128,128]{1,0:T(8,128)(2,1)S(1)}, bf16[128,128]{1,0:T(8,128)(2,1)}, u32[]{:S(2)}) %copy-start.8) | copy-done | bytes 32792
  32.6 5.8 %moves.1 = (f32[1,2,256,128]{3,2,1,0:T(8,128)}, f32[2,1]{1,0:T(2,128)S(1)}) custom-call(f32[2,256,128]{2,1,0:T(8,128)S(1)} %get-tuple-element.4.picked_ref, f32[32,128]{1,0:T(8,128)S(1)} %get-tuple-element.5.total_ref, f32[2,1,2,256,128]{4,3,2,1,0:T(8,128)S(1)} %copy-done.1, s32[2,1]{1,0:T(2,128)S(1)} %copy.13.accept_ref, f32[256,256]{1,0:T(8,128)S(1)} %copy-done.2, ...), custom_call_target="tpu_custom_call" | custom-call | flops 2415919104 | bytes 4194304 | tf_op jit(solution)/shard_map/moves/pallas_call | solution.py:406
  38.4 0.6 %copy.14 = f32[2,1]{0,1:T(1,128)} copy(f32[2,1]{1,0:T(2,128)S(1)} %get-tuple-element.7) | data formatting | bytes 16 | tf_op jit(solution)/shard_map/moves/pallas_call | solution.py:406
Async XLA Ops:
  0.6 0.7 %copy-start.9 = (s32[2,1]{0,1:T(1,128)S(1)}, s32[2,1]{0,1:T(1,128)}, u32[]{:S(2)}) copy-start(s32[2,1]{0,1:T(1,128)} %param.14) | copy-start | bytes 28
  1.4 1.0 %copy-start = (f32[1,2,256,128]{3,2,1,0:T(8,128)S(1)}, f32[1,2,256,128]{3,2,1,0:T(8,128)}, u32[]{:S(2)}) copy-start(f32[1,2,256,128]{3,2,1,0:T(8,128)} %x_ref.1) | copy-start | bytes 786436
  2.4 23.6 %copy-start.2 = (f32[256,256]{1,0:T(8,128)S(1)}, f32[256,256]{1,0:T(8,128)}, u32[]{:S(2)}) copy-start(f32[256,256]{1,0:T(8,128)} %observed_ref.1) | copy-start | bytes 786436
  26.0 1.0 %copy-start.1 = (f32[2,1,2,256,128]{4,3,2,1,0:T(8,128)S(1)}, f32[2,1,2,256,128]{4,3,2,1,0:T(8,128)}, u32[]{:S(2)}) copy-start(f32[2,1,2,256,128]{4,3,2,1,0:T(8,128)} %noise_ref.1) | copy-start | bytes 1572868
  27.0 1.0 %copy-start.3 = (f32[4,256,128]{2,1,0:T(8,128)S(1)}, f32[4,256,128]{2,1,0:T(8,128)}, u32[]{:S(2)}) copy-start(f32[4,256,128]{2,1,0:T(8,128)} %constant.17.clone.scale_ref) | copy-start | bytes 1572868
  28.0 0.9 %copy-start.4 = (bf16[2,256,256]{2,1,0:T(8,128)(2,1)S(1)}, bf16[2,256,256]{2,1,0:T(8,128)(2,1)}, u32[]{:S(2)}) copy-start(bf16[2,256,256]{2,1,0:T(8,128)(2,1)} %constant.15.clone.fore_ref) | copy-start | bytes 786436
  29.0 0.9 %copy-start.5 = (bf16[2,256,256]{2,1,0:T(8,128)(2,1)S(1)}, bf16[2,256,256]{2,1,0:T(8,128)(2,1)}, u32[]{:S(2)}) copy-start(bf16[2,256,256]{2,1,0:T(8,128)(2,1)} %constant.14.clone.back_ref) | copy-start | bytes 786436
  29.9 0.9 %copy-start.6 = (bf16[2,256,256]{2,1,0:T(8,128)(2,1)S(1)}, bf16[2,256,256]{2,1,0:T(8,128)(2,1)}, u32[]{:S(2)}) copy-start(bf16[2,256,256]{2,1,0:T(8,128)(2,1)} %constant.13.clone.unfold_ref) | copy-start | bytes 786436
  30.9 0.9 %copy-start.7 = (bf16[2,256,256]{2,1,0:T(8,128)(2,1)S(1)}, bf16[2,256,256]{2,1,0:T(8,128)(2,1)}, u32[]{:S(2)}) copy-start(bf16[2,256,256]{2,1,0:T(8,128)(2,1)} %constant.12.clone.fold_ref) | copy-start | bytes 786436
  31.8 0.8 %copy-start.8 = (bf16[128,128]{1,0:T(8,128)(2,1)S(1)}, bf16[128,128]{1,0:T(8,128)(2,1)}, u32[]{:S(2)}) copy-start(bf16[128,128]{1,0:T(8,128)(2,1)} %constant.16.clone.flip_ref) | copy-start | bytes 98308
